TPU v7x, 32 devices: a whole 2x2x4 slice. The times are simulated.
32 devices in a mesh: groups: 2 (over y), row: 8 (over z, x), col: 2 (over core).
Axes of the slice: x: 2, y: 2, z: 4, core: 2. Of those that a mesh axis runs over, the one named last changes fastest.
Arguments:
- tokens: bfloat16 [512, 4096], P('groups', 'col'), parts along dimension 0, may hold values from -6 to 6
- teacher: bfloat16 [512, 4096], P(('groups', 'row'), 'col'), parts along dimension 0, may hold values from -3 to 3
- gate_weight: bfloat16 [4096, 16384], P('col', 'row'), may hold values from -0.09375 to 0.09375
- up_weight: bfloat16 [4096, 16384], P('col', 'row'), may hold values from -0.09375 to 0.09375
- down_weight: bfloat16 [16384, 4096], P('row', 'col'), may hold values from -0.046875 to 0.046875
Outputs:
- student_out: bfloat16 [512, 4096], P(('groups', 'row'), 'col'), parts along dimension 0
- d_tokens: bfloat16 [512, 4096], P(('groups', 'row'), 'col'), parts along dimension 0
- grad_gate: bfloat16 [8192, 16384], P(('groups', 'col'), 'row'), parts along dimension 0
- grad_up: bfloat16 [8192, 16384], P(('groups', 'col'), 'row'), parts along dimension 0
- grad_down: bfloat16 [32768, 4096], P(('groups', 'row'), 'col'), parts along dimension 0
There are 2 independent parts, one for each index of `groups`. A program takes and returns all parts, laid end to end along the dimension named above; an argument that names none is the same for every part. Nothing has to cross between parts.
All inputs are finite; a program needn't handle non-finite values.
Results may differ from a plain program's by a relative error of at most 0.0063.
Values may be sent and summed in bfloat16 or wider, within the bound.
A program may use at most 192 MiB of HBM per device.

v0:
```python
import jax
import jax.numpy as jnp
from jax import lax
from jax.sharding import PartitionSpec as P


def local(tokens, teacher, gate_weight, up_weight, down_weight):
    local_rows = teacher.shape[0]
    part_gate = jnp.dot(tokens, gate_weight, preferred_element_type=jnp.float32)
    part_up = jnp.dot(tokens, up_weight, preferred_element_type=jnp.float32)
    gate_proj, up_proj = lax.psum((part_gate, part_up), "col")
    sigmoid_gate = jax.nn.sigmoid(gate_proj)
    activated = gate_proj * sigmoid_gate
    hidden = (activated * up_proj).astype(jnp.bfloat16)
    partial_out = jnp.dot(hidden, down_weight, preferred_element_type=jnp.float32)
    student = lax.psum(partial_out, "row")
    own_start = lax.axis_index("row") * local_rows
    own_rows = lax.dynamic_slice_in_dim(student, own_start, local_rows, 0)
    student_out = own_rows.astype(jnp.bfloat16)
    teacher_all = lax.all_gather(teacher, "row", axis=0, tiled=True)
    d_student = (student - teacher_all.astype(jnp.float32)).astype(jnp.bfloat16)
    hidden_part = lax.dot_general(
        d_student, down_weight, (((1,), (1,)), ((), ())), preferred_element_type=jnp.float32
    )
    d_hidden = lax.psum(hidden_part, "col")
    grad_down = lax.dot_general(
        hidden, d_student, (((0,), (0,)), ((), ())), preferred_element_type=jnp.float32
    ).astype(jnp.bfloat16)
    d_gate = (d_hidden * up_proj * sigmoid_gate * (1.0 + gate_proj * (1.0 - sigmoid_gate))).astype(
        jnp.bfloat16
    )
    d_up = (d_hidden * activated).astype(jnp.bfloat16)
    grad_gate = lax.dot_general(
        tokens, d_gate, (((0,), (0,)), ((), ())), preferred_element_type=jnp.float32
    ).astype(jnp.bfloat16)
    grad_up = lax.dot_general(
        tokens, d_up, (((0,), (0,)), ((), ())), preferred_element_type=jnp.float32
    ).astype(jnp.bfloat16)
    first = lax.dot_general(
        d_gate, gate_weight, (((1,), (1,)), ((), ())), preferred_element_type=jnp.float32
    )
    second = lax.dot_general(
        d_up, up_weight, (((1,), (1,)), ((), ())), preferred_element_type=jnp.float32
    )
    d_tokens = lax.psum_scatter(first + second, "row", scatter_dimension=0, tiled=True).astype(
        jnp.bfloat16
    )
    return (student_out, d_tokens, grad_gate, grad_up, grad_down)


def solution(mesh):
    placed = (
        P("groups", "col"),
        P(("groups", "row"), "col"),
        P("col", "row"),
        P("col", "row"),
        P("row", "col"),
    )
    return jax.shard_map(
        local,
        mesh=mesh,
        in_specs=placed,
        out_specs=(
            P(("groups", "row"), "col"),
            P(("groups", "row"), "col"),
            P(("groups", "col"), "row"),
            P(("groups", "col"), "row"),
            P(("groups", "row"), "col"),
        ),
        check_vma=False,
    )
```

profile of v0, /device:TPU:0, one launch (start us, length us, event | category | flops | bytes accessed | tf_op | source)
XLA Modules:
  0.0 295.2 jit_solution(519798374554103364)
XLA Ops:
  8.1 1.2 copy-done
  9.2 7.0 %fusion.2 = f32[256,2048]{1,0:T(8,128)} fusion(bf16[256,2048]{1,0:T(8,128)(2,1)S(1)} %copy-done, bf16[2048,2048]{1,0:T(8,128)(2,1)} %param.7), kind=kOutput, calls=%fused_computation.12 | convolution fusion | flops 2147483648 | bytes 11534336 | tf_op jit(solution)/shard_map/dot_general | solution.py:9
  16.3 7.0 %fusion.3 = f32[256,2048]{1,0:T(8,128)} fusion(bf16[256,2048]{1,0:T(8,128)(2,1)S(1)} %copy-done, bf16[2048,2048]{1,0:T(8,128)(2,1)} %param.8), kind=kOutput, calls=%fused_computation.13 | convolution fusion | flops 2147483648 | bytes 11534336 | tf_op jit(solution)/shard_map/dot_general | solution.py:10
  23.4 0.5 all-gather.2.cloned.1.call-update
  23.9 30.8 %all-reduce.9.cloned.1.call-done = (f32[256,2048]{1,0:T(8,128)}, f32[256,2048]{1,0:T(8,128)}) async-done(((f32[256,2048]{1,0:T(8,128)}, f32[256,2048]{1,0:T(8,128)}), (f32[256,2048]{1,0:T(8,128)}, f32[256,2048]{1,0:T(8,128)})) %all-reduce.9.cloned.1.call-update) | async-done | bytes 4194320 | tf_op jit(solution)/shard_map/psum | solution.py:11
  54.7 2.8 multiply_convert_fusion.2
  57.6 1.0 copy-done.2
  58.5 7.1 %fusion.4 = f32[256,2048]{1,0:T(8,128)} fusion(bf16[256,2048]{1,0:T(8,128)(2,1)S(1)} %multiply_convert_fusion.2, bf16[2048,2048]{1,0:T(8,128)(2,1)} %param.9), kind=kOutput, calls=%fused_computation.14 | convolution fusion | flops 2147483648 | bytes 11534336 | tf_op jit(solution)/shard_map/dot_general | solution.py:15
  65.7 3.3 %all-gather.2.cloned.1.call-done = bf16[256,2048]{1,0:T(8,128)(2,1)} async-done(((bf16[32,2048]{1,0:T(8,128)(2,1)}), bf16[256,2048]{1,0:T(8,128)(2,1)}) %all-gather.2.cloned.1.call-update) | async-done | bytes 1048592 | tf_op jit(solution)/shard_map/all_gather | solution.py:20
  69.0 105.1 %all-reduce.5.cloned.1.call-done = f32[256,2048]{1,0:T(8,128)} async-done(((f32[256,2048]{1,0:T(8,128)}), f32[256,2048]{1,0:T(8,128)}) %all-reduce.5.cloned.1.call-update) | async-done | bytes 2097168 | tf_op jit(solution)/shard_map/psum | solution.py:16
  174.1 8.0 %fusion.1 = f32[256,2048]{1,0:T(8,128)} fusion(bf16[2048,2048]{1,0:T(8,128)(2,1)} %param.9, f32[256,2048]{1,0:T(8,128)} %all-reduce.5.cloned.1.call-done, bf16[256,2048]{1,0:T(8,128)(2,1)} %all-gather.2.cloned.1.call-done), kind=kOutput, calls=%fused_computation.11 | convolution fusion | flops 2149056512 | bytes 13631488 | tf_op jit(solution)/shard_map/dot_general | solution.py:22
  182.2 0.2 reduce-scatter.2.cloned.1.call-start
  182.4 20.4 %all-reduce.7.cloned.1.call-done = f32[256,2048]{1,0:T(8,128)} async-done(((f32[256,2048]{1,0:T(8,128)}), f32[256,2048]{1,0:T(8,128)}) %all-reduce.7.cloned.1.call-update) | async-done | bytes 2097168 | tf_op jit(solution)/shard_map/psum | solution.py:25
  202.8 3.7 %multiply_convert_fusion = (bf16[256,2048]{1,0:T(8,128)(2,1)S(1)}, bf16[256,2048]{1,0:T(8,128)(2,1)S(1)}) fusion(f32[256,2048]{1,0:T(8,128)} %all-reduce.7.cloned.1.call-done, f32[256,2048]{1,0:T(8,128)} %get-tuple-element.11, f32[256,2048]{1,0:T(8,128)S(1)} %copy-done.1), kind=kLoop, calls=%fused_computation.4 | loop fusion | flops 6815744 | bytes 8388608 | tf_op jit(solution)/shard_map/convert_element_type | solution.py:32
  206.5 6.5 %fusion.5 = f32[256,2048]{1,0:T(8,128)S(1)} fusion(bf16[256,2048]{1,0:T(8,128)(2,1)S(1)} %get-tuple-element.13, bf16[2048,2048]{1,0:T(8,128)(2,1)} %param.7), kind=kOutput, calls=%fused_computation.15 | convolution fusion | flops 2147483648 | bytes 11534336 | tf_op jit(solution)/shard_map/dot_general | solution.py:39
  213.1 3.8 %convolution_add_fusion = f32[256,2048]{1,0:T(8,128)} fusion(f32[256,2048]{1,0:T(8,128)S(1)} %fusion.5, bf16[256,2048]{1,0:T(8,128)(2,1)S(1)} %get-tuple-element.12, bf16[2048,2048]{1,0:T(8,128)(2,1)S(1)} %bitcast.21), kind=kOutput, calls=%fused_computation.3 | convolution fusion | flops 2148007936 | bytes 13631488 | tf_op jit(solution)/shard_map/dot_general | solution.py:42
  216.9 1.8 dynamic-slice_convert_fusion
  218.7 7.5 %convolution_convert_fusion = bf16[2048,2048]{1,0:T(8,128)(2,1)} fusion(bf16[256,2048]{1,0:T(8,128)(2,1)S(1)} %copy-done.3, f32[256,2048]{1,0:T(8,128)} %all-reduce.5.cloned.1.call-done, bf16[256,2048]{1,0:T(8,128)(2,1)S(1)} %copy-done.8), kind=kOutput, calls=%fused_computation.2 | convolution fusion | flops 2153250816 | bytes 12582912 | tf_op jit(solution)/shard_map/dot_general | solution.py:26
  226.2 5.8 %convert_bitcast_fusion.1 = bf16[2048,2048]{0,1:T(8,128)(2,1)} fusion(bf16[256,2048]{1,0:T(8,128)(2,1)S(1)} %copy-done.7, bf16[256,2048]{1,0:T(8,128)(2,1)S(1)} %copy-done), kind=kOutput, calls=%fused_computation.1 | convolution fusion | flops 2151677952 | bytes 10485760 | tf_op jit(solution)/shard_map/dot_general | solution.py:33
  231.9 12.4 %copy.10 = bf16[2048,2048]{1,0:T(8,128)(2,1)} copy(bf16[2048,2048]{0,1:T(8,128)(2,1)} %convert_bitcast_fusion.1) | data formatting | bytes 16777216
  244.3 5.6 %convert_bitcast_fusion = bf16[2048,2048]{0,1:T(8,128)(2,1)} fusion(bf16[256,2048]{1,0:T(8,128)(2,1)S(1)} %copy-done.5, bf16[256,2048]{1,0:T(8,128)(2,1)S(1)} %copy-done), kind=kOutput, calls=%fused_computation | convolution fusion | flops 2151677952 | bytes 10485760 | tf_op jit(solution)/shard_map/dot_general | solution.py:36
  249.9 12.2 %copy.11 = bf16[2048,2048]{1,0:T(8,128)(2,1)} copy(bf16[2048,2048]{0,1:T(8,128)(2,1)} %convert_bitcast_fusion) | data formatting | bytes 16777216
  262.2 23.9 %reduce-scatter.2.cloned.1.call-done = f32[32,2048]{1,0:T(8,128)} async-done(((f32[256,2048]{1,0:T(8,128)}), f32[32,2048]{1,0:T(8,128)}) %reduce-scatter.2.cloned.1.call-update) | async-done | bytes 262160 | tf_op jit(solution)/shard_map/reduce_scatter | solution.py:45
  286.0 1.6 convert_element_type.42
  (29 shorter events, 0.3 us)
Async XLA Ops:
  8.0 1.2 copy-start
  8.0 46.7 %all-reduce.9.cloned.1.call-start = ((), (), s32[]{:S(2)}) async-start(), calls=%async_computation.5 | async-start | bytes 8388608 | tf_op jit(solution)/shard_map/psum | solution.py:11
  23.3 45.7 %all-gather.2.cloned.1.call-start = ((), (), s32[]{:S(2)}) async-start(), calls=%async_computation.2 | async-start | bytes 1179648 | tf_op jit(solution)/shard_map/all_gather | solution.py:20
  23.9 150.2 %all-reduce.5.cloned.1.call-start = ((), (), s32[]{:S(2)}) async-start(), calls=%async_computation.1 | async-start | bytes 4194304 | tf_op jit(solution)/shard_map/psum | solution.py:16
  57.6 1.0 copy-start.2
  65.6 137.2 %all-reduce.7.cloned.1.call-start = ((), (), s32[]{:S(2)}) async-start(), calls=%async_computation.3 | async-start | bytes 4194304 | tf_op jit(solution)/shard_map/psum | solution.py:25
  182.2 20.6 %copy-start.1 = (f32[256,2048]{1,0:T(8,128)S(1)}, f32[256,2048]{1,0:T(8,128)}, u32[]{:S(2)}) copy-start(f32[256,2048]{1,0:T(8,128)} %get-tuple-element.10) | copy-start | bytes 6291460
  182.2 103.8 %reduce-scatter.2.cloned.1.call-start = ((), (), s32[]{:S(2)}) async-start(), calls=%async_computation.4 | async-start | bytes 2359296 | tf_op jit(solution)/shard_map/reduce_scatter | solution.py:45
  202.8 10.3 %slice-start = ((s8[8388608]{0:T(1024)(128)(4,1)}), s8[4194304]{0:T(1024)(128)(4,1)S(1)}, s32[]{:S(2)}) async-start(s8[8388608]{0:T(1024)(128)(4,1)} %bitcast.20), calls=%async_computation.6 | async-start | bytes 8388608
  206.5 6.6 %copy-start.6 = (bf16[256,2048]{1,0:T(8,128)(2,1)}, bf16[256,2048]{1,0:T(8,128)(2,1)S(1)}, u32[]{:S(2)}) copy-start(bf16[256,2048]{1,0:T(8,128)(2,1)S(1)} %get-tuple-element.13) | copy-start | bytes 3145732
  206.5 6.6 %copy-start.4 = (bf16[256,2048]{1,0:T(8,128)(2,1)}, bf16[256,2048]{1,0:T(8,128)(2,1)S(1)}, u32[]{:S(2)}) copy-start(bf16[256,2048]{1,0:T(8,128)(2,1)S(1)} %get-tuple-element.12) | copy-start | bytes 3145732
  206.5 6.6 %slice-start.1 = ((s8[8388608]{0:T(1024)(128)(4,1)}), s8[4194304]{0:T(1024)(128)(4,1)S(1)}, s32[]{:S(2)}) async-start(s8[8388608]{0:T(1024)(128)(4,1)} %bitcast.20), calls=%async_computation.7 | async-start | bytes 8388608
  216.9 1.8 copy-start.3
  216.9 1.8 copy-start.8
  218.7 7.5 %copy-start.7 = (bf16[256,2048]{1,0:T(8,128)(2,1)S(1)}, bf16[256,2048]{1,0:T(8,128)(2,1)}, u32[]{:S(2)}) copy-start(bf16[256,2048]{1,0:T(8,128)(2,1)} %copy-done.6) | copy-start | bytes 3145732
  231.9 12.4 %copy-start.5 = (bf16[256,2048]{1,0:T(8,128)(2,1)S(1)}, bf16[256,2048]{1,0:T(8,128)(2,1)}, u32[]{:S(2)}) copy-start(bf16[256,2048]{1,0:T(8,128)(2,1)} %copy-done.4) | copy-start | bytes 3145732
Sparse Core Ops, SparseCore 0:
  23.4 31.2 all-reduce.8
  182.3 20.4 all-reduce.6
Sparse Core Ops, SparseCore 1:
  25.9 43.1 all-gather.1
  73.5 100.6 all-reduce.4
  217.0 69.0 reduce-scatter.1
where the time goes:
time: 296 us; the launch traced here: 295 us
  waiting for transfers between devices  184 us (62%)
  matrix products  58.3 us (20%)
  local copies, waits for them, and re-layouts  28.6 us (10%)
  between operations  15.8 us (5%)
  other arithmetic  8.11 us (3%)
    psum x1, waiting for transfers between devices, local(): student = lax.psum(partial_out, 'row')  105 us
    psum x1, waiting for transfers between devices, local(): gate_proj, up_proj = lax.psum((part_gate, part_up), 'col')  30.8 us
    unnamed x24, local copies, waits for them, and re-layouts  26.8 us
    reduce_scatter x1, waiting for transfers between devices, local(): lax.psum_scatter(first + second, 'row', scatter_dimension=0, tiled=True)  23.9 us
    psum x1, waiting for transfers between devices, local(): d_hidden = lax.psum(hidden_part, 'col')  20.4 us
    dot_general x1, matrix products, local(): lax.dot_general(d_student, down_weight, (((1,), (1,)), ((), ())), preferr...  8.04 us
    dot_general x1, matrix products, local(): lax.dot_general(hidden, d_student, (((0,), (0,)), ((), ())), preferred_el...  7.47 us
    dot_general x1, matrix products, local(): jnp.dot(hidden, down_weight, preferred_element_type=jnp.float32)  7.08 us
  transfers between devices with their start and end apart: 5, of which 5 were waited for; matrix products, arithmetic and copies ran while one was open for 19% of the time, Pallas kernels for 0%

commit v1 on v0

v1 whole, which is shorter than its diff:
```python
import jax
import jax.numpy as jnp
from jax import lax
from jax.experimental import pallas as pl
from jax.experimental.pallas import tpu as pltpu
from jax.sharding import PartitionSpec as P

F32 = jnp.float32
BF = jnp.bfloat16
MESH = pl.DeviceIdType.MESH
FCH = 256
NC = 4
ORDER = ("A0", "A1", "A2", "B0", "A3", "B1", "C0", "B2", "C1", "B3", "C2", "C3")


def nt(a, b):
    return lax.dot_general(a, b, (((1,), (1,)), ((), ())), preferred_element_type=F32)


def tn(a, b):
    return lax.dot_general(a, b, (((0,), (0,)), ((), ())), preferred_element_type=F32)


def kernel(
    tokens_h, teacher_ref, wg_h, wu_h, wd_h,
    out_ref, dtok_ref, hid_h, ds_h, dg_h, du_h,
    tok, wg, wu, wd, gp, up, gus, gur, hid,
    pf, pb, xr, sf, zs, za, zb, dsf, dh, dhs, dhr, dg, du,
    pf2, pb2, xr2, zs2, za2, zb2,
    ld_tok, ld_g, ld_u, ld_d, st,
    gu_ss, gu_rs, dh_ss, dh_rs,
    x_ss, x_rs, za_ss, za_rs, zb_ss, zb_rs, ze_ss, ze_rs,
    agz_ss, agz_rs, agm_ss, agx_ss, agx_rs,
):
    r = lax.axis_index("row")
    core = lax.axis_index("col")
    z = r // 2
    x = r % 2
    hi = z // 2
    is_end = jnp.logical_or(z == 0, z == 3)
    is_mid = jnp.logical_not(is_end)
    nz = z + 1 - 2 * (z % 2)
    xid = {"row": z * 2 + 1 - x}
    nid = {"row": nz * 2 + x}
    mid = {"row": (3 - z) * 2 + x}
    cid = {"col": 1 - core}
    end_b = 3 * hi
    far = 2 - 2 * hi
    near = 2 * hi
    three = 1 - hi
    far_m = 2 - hi
    far_e = 3 - 3 * hi
    nff = wg.shape[1]
    nd = wd.shape[1]
    nj = nff // FCH
    cw = nd // NC
    dcw = wg.shape[0] // NC

    def fcols(j):
        return pl.ds(pl.multiple_of(j * FCH, FCH), FCH)

    def cols(c):
        return pl.ds(c * cw, cw)

    pltpu.make_async_copy(tokens_h, tok, ld_tok).start()
    for j in range(nj):
        s = pl.ds(j * FCH, FCH)
        pltpu.make_async_copy(wg_h.at[:, s], wg.at[:, s], ld_g.at[j]).start()
        pltpu.make_async_copy(wu_h.at[:, s], wu.at[:, s], ld_u.at[j]).start()
    for c in range(NC):
        pltpu.make_async_copy(wd_h.at[:, cols(c)], wd.at[:, cols(c)], ld_d.at[c]).start()

    barrier = pltpu.get_barrier_semaphore()
    pl.semaphore_signal(barrier, inc=1, device_id=cid, device_id_type=MESH)
    pl.semaphore_signal(barrier, inc=1, device_id=xid, device_id_type=MESH)
    pl.semaphore_signal(barrier, inc=1, device_id=nid, device_id_type=MESH)

    @pl.when(is_mid)
    def _():
        pl.semaphore_signal(barrier, inc=1, device_id=mid, device_id_type=MESH)
        pl.semaphore_wait(barrier, 4)

    @pl.when(is_end)
    def _():
        pl.semaphore_wait(barrier, 3)

    def rc(src, dst, ss, rs, dev):
        return pltpu.make_async_remote_copy(
            src_ref=src, dst_ref=dst, send_sem=ss, recv_sem=rs, device_id=dev, device_id_type=MESH
        )

    def gu_copy(j):
        return rc(gus.at[j], gur.at[j], gu_ss.at[j], gu_rs.at[j], cid)

    pltpu.make_async_copy(tokens_h, tok, ld_tok).wait()

    def first(j, carry):
        s = fcols(j)
        pltpu.make_async_copy(wg_h.at[:, s], wg.at[:, s], ld_g.at[j]).wait()
        pg = jnp.dot(tok[...], wg[:, s], preferred_element_type=F32)
        gp[:, s] = pg
        gus[j, 0] = pg.astype(BF)
        pltpu.make_async_copy(wu_h.at[:, s], wu.at[:, s], ld_u.at[j]).wait()
        pu = jnp.dot(tok[...], wu[:, s], preferred_element_type=F32)
        up[:, s] = pu
        gus[j, 1] = pu.astype(BF)
        gu_copy(j).start()
        return carry

    lax.fori_loop(0, nj, first, 0)

    def second(j, carry):
        s = fcols(j)
        gu_copy(j).wait_recv()
        g = gp[:, s] + gur[j, 0].astype(F32)
        u = up[:, s] + gur[j, 1].astype(F32)
        gp[:, s] = g
        up[:, s] = u
        hid[:, s] = (g * jax.nn.sigmoid(g) * u).astype(BF)
        return carry

    lax.fori_loop(0, nj, second, 0)
    pltpu.make_async_copy(hid, hid_h, st.at[0]).start()

    def x_copy(k, c):
        b, t = (pb, xr) if k == 0 else (pb2, xr2)
        return rc(b.at[:, 1 - x, :, cols(c)], t.at[:, :, cols(c)], x_ss.at[k, c], x_rs.at[k, c], xid)

    def in_copy(k, c):
        b, t = (zs, za) if k == 0 else (zs2, za2)
        return rc(b.at[pl.ds(three, 3), :, cols(c)], t.at[pl.ds(three, 3), :, cols(c)], za_ss.at[k, c], za_rs.at[k, c], nid)

    def mid_copy(k, c, start):
        b, t = (zs, zb) if k == 0 else (zs2, zb2)
        return rc(b.at[pl.ds(start, 2), :, cols(c)], t.at[pl.ds(start, 2), :, cols(c)], zb_ss.at[k, c], zb_rs.at[k, c], mid)

    def out_copy(k, c):
        b, t = (zs, za) if k == 0 else (zs2, za2)
        return rc(b.at[pl.ds(end_b, 1), :, cols(c)], t.at[pl.ds(end_b, 1), :, cols(c)], ze_ss.at[k, c], ze_rs.at[k, c], nid)

    def stage_a(k, c):
        f, t = (pf, xr) if k == 0 else (pf2, xr2)
        b, a = (zs, za) if k == 0 else (zs2, za2)
        q = cols(c)
        x_copy(k, c).wait_recv()
        sf[:, :, q] = f[:, x, :, q] + t[:, :, q].astype(F32)

        @pl.when(is_end)
        def _():
            b[pl.ds(three, 3), :, q] = sf[pl.ds(three, 3), :, q].astype(BF)
            in_copy(k, c).start()

        @pl.when(is_mid)
        def _():
            in_copy(k, c).wait_recv()
            m = pl.ds(far, 2)
            b[m, :, q] = (sf[m, :, q] + a[m, :, q].astype(F32)).astype(BF)
            mid_copy(k, c, far).start()

    def stage_b(k, c, final):
        b, a, m = (zs, za, zb) if k == 0 else (zs2, za2, zb2)
        q = cols(c)

        @pl.when(is_end)
        def _():
            out_copy(k, c).wait_recv()
            final(c, sf[z, :, q] + a[z, :, q].astype(F32))

        @pl.when(is_mid)
        def _():
            mid_copy(k, c, near).wait_recv()
            b[end_b, :, q] = (sf[end_b, :, q] + m[end_b, :, q].astype(F32)).astype(BF)
            out_copy(k, c).start()
            final(c, sf[z, :, q] + a[z, :, q].astype(F32) + m[z, :, q].astype(F32))

    def rs_drain(k):
        for c in range(NC):
            x_copy(k, c).wait_send()

            @pl.when(is_end)
            def _():
                in_copy(k, c).wait_send()

            @pl.when(is_mid)
            def _():
                mid_copy(k, c, far).wait_send()
                out_copy(k, c).wait_send()

    for c in range(NC):
        q = cols(c)
        pltpu.make_async_copy(wd_h.at[:, q], wd.at[:, q], ld_d.at[c]).wait()
        pc = jnp.dot(hid[...], wd[:, q], preferred_element_type=F32).reshape(4, 2, 32, cw)
        pf[:, :, :, q] = pc
        pb[:, :, :, q] = pc.astype(BF)
        x_copy(0, c).start()

    def factors(j, carry):
        s = fcols(j)
        g = gp[:, s]
        u = up[:, s]
        sg = jax.nn.sigmoid(g)
        gp[:, s] = u * sg * (1.0 + g * (1.0 - sg))
        up[:, s] = g * sg
        return carry

    lax.fori_loop(0, nj, factors, 0)

    def agz(c, t):
        b = dsf.at[t * 2 + x, :, cols(c)]
        return rc(b, b, agz_ss.at[c, t], agz_rs.at[c, t], nid)

    def agm(c, t):
        b = dsf.at[t * 2 + x, :, cols(c)]
        return rc(b, b, agm_ss.at[c, t], agz_rs.at[c, t], mid)

    def agx(c, t, src_x):
        b = dsf.at[t * 2 + src_x, :, cols(c)]
        return rc(b, b, agx_ss.at[c, t], agx_rs.at[c, t], xid)

    def student_final(c, v):
        q = cols(c)
        out_ref[:, q] = v.astype(BF)
        dsf[r, :, q] = (v - teacher_ref[:, q].astype(F32)).astype(BF)
        agz(c, z).start()
        pl.when(is_mid)(lambda: agm(c, z).start())
        agx(c, z, x).start()

    def stage_c(c):
        @pl.when(is_end)
        def _():
            agz(c, nz).wait_recv()
            agx(c, nz, x).start()
            agz(c, far_m).wait_recv()
            agx(c, far_m, x).start()
            agz(c, far_e).wait_recv()
            agx(c, far_e, x).start()

        @pl.when(is_mid)
        def _():
            agz(c, nz).wait_recv()
            agm(c, nz).start()
            agx(c, nz, x).start()
            agm(c, far_m).wait_recv()
            agz(c, far_m).start()
            agx(c, far_m, x).start()
            agm(c, far_e).wait_recv()
            agz(c, far_e).start()
            agx(c, far_e, x).start()

    for step in ORDER:
        c = int(step[1])
        if step[0] == "A":
            stage_a(0, c)
        elif step[0] == "B":
            stage_b(0, c, student_final)
        else:
            stage_c(c)
    for c in range(NC):
        for t in range(4):
            agx(c, t, 1 - x).wait_recv()
    ds_copy = pltpu.make_async_copy(dsf, ds_h, st.at[1])
    ds_copy.start()

    def dh_copy(j):
        return rc(dhs.at[j], dhr.at[j], dh_ss.at[j], dh_rs.at[j], cid)

    def third(j, carry):
        p = nt(dsf[...].reshape(256, nd), wd[fcols(j), :])
        dh[j] = p
        dhs[j] = p.astype(BF)
        dh_copy(j).start()
        return carry

    lax.fori_loop(0, nj, third, 0)

    def fourth(j, carry):
        s = fcols(j)
        dh_copy(j).wait_recv()
        d = dh[j] + dhr[j].astype(F32)
        dg[:, s] = (d * gp[:, s]).astype(BF)
        du[:, s] = (d * up[:, s]).astype(BF)
        return carry

    lax.fori_loop(0, nj, fourth, 0)
    pltpu.make_async_copy(dg, dg_h, st.at[2]).start()
    pltpu.make_async_copy(du, du_h, st.at[3]).start()

    for c in range(NC):
        q = cols(c)
        pc = (nt(dg[...], wg[q, :]) + nt(du[...], wu[q, :])).reshape(4, 2, 32, cw)
        pf2[:, :, :, q] = pc
        pb2[:, :, :, q] = pc.astype(BF)
        x_copy(1, c).start()

    def dtok_final(c, v):
        dtok_ref[:, cols(c)] = v.astype(BF)

    for step in ORDER:
        c = int(step[1])
        if step[0] == "A":
            stage_a(1, c)
        elif step[0] == "B":
            stage_b(1, c, dtok_final)

    def drain(j, carry):
        gu_copy(j).wait_send()
        dh_copy(j).wait_send()
        return carry

    lax.fori_loop(0, nj, drain, 0)
    rs_drain(0)
    rs_drain(1)
    for c in range(NC):
        agz(c, z).wait_send()
        for t in range(4):
            agx(c, t, x).wait_send()

        @pl.when(is_mid)
        def _():
            agm(c, z).wait_send()
            agm(c, nz).wait_send()
            agz(c, far_m).wait_send()
            agz(c, far_e).wait_send()

    for i, (a, b) in enumerate(((hid, hid_h), (dsf, ds_h), (dg, dg_h), (du, du_h))):
        pltpu.make_async_copy(a, b, st.at[i]).wait()


def fused(tokens, teacher, gate_weight, up_weight, down_weight):
    m, d = tokens.shape
    ff = gate_weight.shape[1]
    rows = teacher.shape[0]
    nj = ff // FCH
    V = pltpu.VMEM
    D = pltpu.SemaphoreType.DMA
    rs_set = [V((4, rows, d), BF)] * 3
    scratch = [
        V((m, d), BF), V((d, ff), BF), V((d, ff), BF), V((ff, d), BF),
        V((m, ff), F32), V((m, ff), F32),
        V((nj, 2, m, FCH), BF), V((nj, 2, m, FCH), BF), V((m, ff), BF),
        V((4, 2, rows, d), F32), V((4, 2, rows, d), BF), V((4, rows, d), BF), V((4, rows, d), F32),
        *rs_set, V((8, rows, d), BF),
        V((nj, m, FCH), F32), V((nj, m, FCH), BF), V((nj, m, FCH), BF),
        V((m, ff), BF), V((m, ff), BF),
        V((4, 2, rows, d), F32), V((4, 2, rows, d), BF), V((4, rows, d), BF), *rs_set,
        D, D((nj,)), D((nj,)), D((NC,)), D((4,)),
        D((nj,)), D((nj,)), D((nj,)), D((nj,)),
        *([D((2, NC))] * 8),
        *([D((NC, 4))] * 5),
    ]
    hbm = pl.BlockSpec(memory_space=pl.ANY)
    vm = pl.BlockSpec(memory_space=pltpu.VMEM)
    flops = 2 * m * d * ff * 6
    return pl.pallas_call(
        kernel,
        out_shape=(
            jax.ShapeDtypeStruct((rows, d), BF), jax.ShapeDtypeStruct((rows, d), BF),
            jax.ShapeDtypeStruct((m, ff), BF), jax.ShapeDtypeStruct((8, rows, d), BF),
            jax.ShapeDtypeStruct((m, ff), BF), jax.ShapeDtypeStruct((m, ff), BF),
        ),
        in_specs=[hbm, vm, hbm, hbm, hbm],
        out_specs=(vm, vm, hbm, hbm, hbm, hbm),
        scratch_shapes=scratch,
        compiler_params=pltpu.CompilerParams(
            collective_id=0, has_side_effects=True, vmem_limit_bytes=62 * 1024 * 1024
        ),
        cost_estimate=pl.CostEstimate(flops=flops, bytes_accessed=6 * d * ff, transcendentals=m * ff),
        name="chain",
    )(tokens, teacher, gate_weight, up_weight, down_weight)


def local_fused(tokens, teacher, gate_weight, up_weight, down_weight):
    out, dtok, hid, ds, dg, du = fused(tokens, teacher, gate_weight, up_weight, down_weight)
    ds = ds.reshape(tokens.shape)
    grad_down = tn(hid, ds).astype(BF)
    grad_gate = tn(tokens, dg).astype(BF)
    grad_up = tn(tokens, du).astype(BF)
    return out, dtok, grad_gate, grad_up, grad_down


def local(tokens, teacher, gate_weight, up_weight, down_weight):
    local_rows = teacher.shape[0]
    part_gate = jnp.dot(tokens, gate_weight, preferred_element_type=F32)
    part_up = jnp.dot(tokens, up_weight, preferred_element_type=F32)
    gate_proj, up_proj = lax.psum((part_gate, part_up), "col")
    sigmoid_gate = jax.nn.sigmoid(gate_proj)
    activated = gate_proj * sigmoid_gate
    hidden = (activated * up_proj).astype(BF)
    partial_out = jnp.dot(hidden, down_weight, preferred_element_type=F32)
    student = lax.psum(partial_out, "row")
    own_start = lax.axis_index("row") * local_rows
    own_rows = lax.dynamic_slice_in_dim(student, own_start, local_rows, 0)
    student_out = own_rows.astype(BF)
    teacher_all = lax.all_gather(teacher, "row", axis=0, tiled=True)
    d_student = (student - teacher_all.astype(F32)).astype(BF)
    d_hidden = lax.psum(nt(d_student, down_weight), "col")
    grad_down = tn(hidden, d_student).astype(BF)
    d_gate = (d_hidden * up_proj * sigmoid_gate * (1.0 + gate_proj * (1.0 - sigmoid_gate))).astype(BF)
    d_up = (d_hidden * activated).astype(BF)
    grad_gate = tn(tokens, d_gate).astype(BF)
    grad_up = tn(tokens, d_up).astype(BF)
    total = nt(d_gate, gate_weight) + nt(d_up, up_weight)
    d_tokens = lax.psum_scatter(total, "row", scatter_dimension=0, tiled=True).astype(BF)
    return (student_out, d_tokens, grad_gate, grad_up, grad_down)


def solution(mesh):
    placed = (
        P("groups", "col"),
        P(("groups", "row"), "col"),
        P("col", "row"),
        P("col", "row"),
        P("row", "col"),
    )
    small = mesh.shape["row"] == 8 and mesh.shape["col"] == 2
    return jax.shard_map(
        local_fused if small else local,
        mesh=mesh,
        in_specs=placed,
        out_specs=(
            P(("groups", "row"), "col"),
            P(("groups", "row"), "col"),
            P(("groups", "col"), "row"),
            P(("groups", "col"), "row"),
            P(("groups", "row"), "col"),
        ),
        check_vma=False,
    )
```

time: 296 us -> 154 us (0.52)
  waiting for transfers between devices: 184 us -> 0 us
  Pallas kernels: 0 us -> 108 us
  matrix products: 58.3 us -> 18.6 us
  between operations: 15.8 us -> 0.68 us
  other arithmetic: 8.11 us -> 0 us
    psum x3 -> x0, waiting for transfers between devices: 156 us -> none  [the longest x1 105 us: local(): student = lax.psum(partial_out, 'row')]
    pallas_call x0 -> x1, Pallas kernels: none -> 108 us  [fused(): pl.pallas_call(kernel, out_shape=(jax.ShapeDtypeStruct((rows, d), BF), ja...]
    dot_general x9 -> x3, matrix products: 58.3 us -> 18.6 us  [tn(): lax.dot_general(a, b, (((0,), (0,)), ((), ())), preferred_element_type=F32)]
    reduce_scatter x1 -> x0, waiting for transfers between devices: 23.9 us -> none  [local(): lax.psum_scatter(first + second, 'row', scatter_dimension=0, tiled=True)]
    convert_element_type x3 -> x0, other arithmetic: 8.11 us -> none  [the longest x1 3.66 us: local(): d_up = (d_hidden * activated).astype(jnp.bfloat16)]
    all_gather x1 -> x0, waiting for transfers between devices: 3.35 us -> none  [local(): teacher_all = lax.all_gather(teacher, 'row', axis=0, tiled=True)]
    unnamed x24 -> x16, local copies, waits for them, and re-layouts: 26.8 us -> 26 us
  transfers between devices with their start and end apart: 5 -> 0, of which waited for: 5 -> 0; matrix products, arithmetic and copies ran while one was open for 19% -> 0% of each run, Pallas kernels for 0% -> 0%
where the time goes in v1:
time: 154 us; the launch traced here: 153 us
  Pallas kernels  108 us (70%)
  local copies, waits for them, and re-layouts  26 us (17%)
  matrix products  18.6 us (12%)
    pallas_call x1, Pallas kernels, fused(): pl.pallas_call(kernel, out_shape=(jax.ShapeDtypeStruct((rows, d), BF), ja...  108 us
    unnamed x16, local copies, waits for them, and re-layouts  26 us
    dot_general x3, matrix products, tn(): lax.dot_general(a, b, (((0,), (0,)), ((), ())), preferred_element_type=F32)  18.6 us

profile of v1, /device:TPU:0, one launch (start us, length us, event | category | flops | bytes accessed | tf_op | source)
XLA Modules:
  0.0 153.3 jit_solution(9308541975025051195)
XLA Ops:
  0.6 0.0 copy-start
  0.6 108.1 %chain.1 = (bf16[32,2048]{1,0:T(8,128)(2,1)}, bf16[32,2048]{1,0:T(8,128)(2,1)}, bf16[256,2048]{1,0:T(8,128)(2,1)}, bf16[8,32,2048]{2,1,0:T(8,128)(2,1)}, bf16[25...) custom-call(bf16[256,2048]{1,0:T(8,128)(2,1)} %tokens_h.1, bf16[32,2048]{1,0:T(8,128)(2,1)} %teacher_ref.1, ...), custom_call_target="tpu_custom_call" | custom-call | flops 12884901888 | bytes 25165824 | tf_op jit(solution)/shard_map/chain/pallas_call | solution.py:354
  108.7 0.0 copy-done
  108.7 7.0 %convert_bitcast_fusion.1 = bf16[2048,2048]{0,1:T(8,128)(2,1)} fusion(bf16[256,2048]{1,0:T(8,128)(2,1)} %get-tuple-element.13, bf16[256,2048]{1,0:T(8,128)(2,1)S(1)} %copy-done), kind=kOutput, calls=%fused_computation.1 | convolution fusion | flops 2151677952 | bytes 10485760 | tf_op jit(solution)/shard_map/dot_general | solution.py:21
  115.7 0.0 copy-start.2
  115.7 12.3 %copy.10 = bf16[2048,2048]{1,0:T(8,128)(2,1)} copy(bf16[2048,2048]{0,1:T(8,128)(2,1)} %convert_bitcast_fusion.1) | data formatting | bytes 16777216
  128.0 0.0 copy-done.2
  128.0 5.8 %convert_bitcast_fusion = bf16[2048,2048]{0,1:T(8,128)(2,1)} fusion(bf16[256,2048]{1,0:T(8,128)(2,1)S(1)} %copy-done.2, bf16[256,2048]{1,0:T(8,128)(2,1)S(1)} %copy-done), kind=kOutput, calls=%fused_computation | convolution fusion | flops 2151677952 | bytes 10485760 | tf_op jit(solution)/shard_map/dot_general | solution.py:21
  133.8 0.0 copy-start.1
  133.8 0.0 copy-start.3
  133.8 12.4 %copy.11 = bf16[2048,2048]{1,0:T(8,128)(2,1)} copy(bf16[2048,2048]{0,1:T(8,128)(2,1)} %convert_bitcast_fusion) | data formatting | bytes 16777216
  146.2 0.0 copy-done.1
  146.2 0.0 copy-done.3
  146.2 0.0 copy-start.5
  146.2 0.0 copy-start.4
  146.2 5.8 %convolution_convert_fusion = bf16[2048,2048]{1,0:T(8,128)(2,1)} fusion(bf16[256,2048]{1,0:T(8,128)(2,1)S(1)} %copy-done.1, bf16[256,2048]{1,0:T(8,128)(2,1)S(1)} %bitcast.11), kind=kOutput, calls=%fused_computation.2 | convolution fusion | flops 2151677952 | bytes 10485760 | tf_op jit(solution)/shard_map/dot_general | solution.py:21
  152.0 0.0 copy-done.5
  152.0 0.7 copy.14
  152.7 0.0 copy-done.4
  152.7 0.7 copy.15
Async XLA Ops:
  0.6 108.1 %copy-start = (bf16[256,2048]{1,0:T(8,128)(2,1)S(1)}, bf16[256,2048]{1,0:T(8,128)(2,1)}, u32[]{:S(2)}) copy-start(bf16[256,2048]{1,0:T(8,128)(2,1)} %tokens_h.1) | copy-start | bytes 3145732
  115.7 12.3 %copy-start.2 = (bf16[256,2048]{1,0:T(8,128)(2,1)S(1)}, bf16[256,2048]{1,0:T(8,128)(2,1)}, u32[]{:S(2)}) copy-start(bf16[256,2048]{1,0:T(8,128)(2,1)} %get-tuple-element.14) | copy-start | bytes 3145732
  133.8 12.4 %copy-start.1 = (bf16[256,2048]{1,0:T(8,128)(2,1)S(1)}, bf16[256,2048]{1,0:T(8,128)(2,1)}, u32[]{:S(2)}) copy-start(bf16[256,2048]{1,0:T(8,128)(2,1)} %get-tuple-element.15) | copy-start | bytes 3145732
  133.8 12.4 %copy-start.3 = (bf16[8,32,2048]{2,1,0:T(8,128)(2,1)S(1)}, bf16[8,32,2048]{2,1,0:T(8,128)(2,1)}, u32[]{:S(2)}) copy-start(bf16[8,32,2048]{2,1,0:T(8,128)(2,1)} %get-tuple-element.16) | copy-start | bytes 3145732
  146.2 5.8 %copy-start.5 = (bf16[32,2048]{1,0:T(8,128)(2,1)S(1)}, bf16[32,2048]{1,0:T(8,128)(2,1)}, u32[]{:S(2)}) copy-start(bf16[32,2048]{1,0:T(8,128)(2,1)} %get-tuple-element.27) | copy-start | bytes 393220
  146.2 6.5 %copy-start.4 = (bf16[32,2048]{1,0:T(8,128)(2,1)S(1)}, bf16[32,2048]{1,0:T(8,128)(2,1)}, u32[]{:S(2)}) copy-start(bf16[32,2048]{1,0:T(8,128)(2,1)} %get-tuple-element.28) | copy-start | bytes 393220

commit v2 on v1

--- a/solution.py
+++ b/solution.py
@@ -8,9 +8,10 @@
 F32 = jnp.float32
 BF = jnp.bfloat16
 MESH = pl.DeviceIdType.MESH
-FCH = 256
+FCH = 512
 NC = 4
-ORDER = ("A0", "A1", "A2", "B0", "A3", "B1", "C0", "B2", "C1", "B3", "C2", "C3")
+LAG_B = 1
+LAG_C = 2
 
 
 def nt(a, b):
@@ -25,31 +26,19 @@
     tokens_h, teacher_ref, wg_h, wu_h, wd_h,
     out_ref, dtok_ref, hid_h, ds_h, dg_h, du_h,
     tok, wg, wu, wd, gp, up, gus, gur, hid,
-    pf, pb, xr, sf, zs, za, zb, dsf, dh, dhs, dhr, dg, du,
-    pf2, pb2, xr2, zs2, za2, zb2,
+    pf, pb, xr, sf, zs, zr, dsf, dh, dhs, dhr, dg, du,
+    pf2, pb2, xr2, zs2, zr2,
     ld_tok, ld_g, ld_u, ld_d, st,
     gu_ss, gu_rs, dh_ss, dh_rs,
-    x_ss, x_rs, za_ss, za_rs, zb_ss, zb_rs, ze_ss, ze_rs,
-    agz_ss, agz_rs, agm_ss, agx_ss, agx_rs,
+    x_ss, x_rs, z_ss, z_rs, agz_ss, agz_rs, agx_ss, agx_rs,
 ):
     r = lax.axis_index("row")
     core = lax.axis_index("col")
     z = r // 2
     x = r % 2
-    hi = z // 2
-    is_end = jnp.logical_or(z == 0, z == 3)
-    is_mid = jnp.logical_not(is_end)
-    nz = z + 1 - 2 * (z % 2)
     xid = {"row": z * 2 + 1 - x}
-    nid = {"row": nz * 2 + x}
-    mid = {"row": (3 - z) * 2 + x}
     cid = {"col": 1 - core}
-    end_b = 3 * hi
-    far = 2 - 2 * hi
-    near = 2 * hi
-    three = 1 - hi
-    far_m = 2 - hi
-    far_e = 3 - 3 * hi
+    others = [(z + i) % 4 for i in (1, 2, 3)]
     nff = wg.shape[1]
     nd = wd.shape[1]
     nj = nff // FCH
@@ -73,16 +62,9 @@
     barrier = pltpu.get_barrier_semaphore()
     pl.semaphore_signal(barrier, inc=1, device_id=cid, device_id_type=MESH)
     pl.semaphore_signal(barrier, inc=1, device_id=xid, device_id_type=MESH)
-    pl.semaphore_signal(barrier, inc=1, device_id=nid, device_id_type=MESH)
-
-    @pl.when(is_mid)
-    def _():
-        pl.semaphore_signal(barrier, inc=1, device_id=mid, device_id_type=MESH)
-        pl.semaphore_wait(barrier, 4)
-
-    @pl.when(is_end)
-    def _():
-        pl.semaphore_wait(barrier, 3)
+    for t in others:
+        pl.semaphore_signal(barrier, inc=1, device_id={"row": t * 2 + x}, device_id_type=MESH)
+    pl.semaphore_wait(barrier, 5)
 
     def rc(src, dst, ss, rs, dev):
         return pltpu.make_async_remote_copy(
@@ -126,65 +108,38 @@
         b, t = (pb, xr) if k == 0 else (pb2, xr2)
         return rc(b.at[:, 1 - x, :, cols(c)], t.at[:, :, cols(c)], x_ss.at[k, c], x_rs.at[k, c], xid)
 
-    def in_copy(k, c):
-        b, t = (zs, za) if k == 0 else (zs2, za2)
-        return rc(b.at[pl.ds(three, 3), :, cols(c)], t.at[pl.ds(three, 3), :, cols(c)], za_ss.at[k, c], za_rs.at[k, c], nid)
-
-    def mid_copy(k, c, start):
-        b, t = (zs, zb) if k == 0 else (zs2, zb2)
-        return rc(b.at[pl.ds(start, 2), :, cols(c)], t.at[pl.ds(start, 2), :, cols(c)], zb_ss.at[k, c], zb_rs.at[k, c], mid)
-
-    def out_copy(k, c):
-        b, t = (zs, za) if k == 0 else (zs2, za2)
-        return rc(b.at[pl.ds(end_b, 1), :, cols(c)], t.at[pl.ds(end_b, 1), :, cols(c)], ze_ss.at[k, c], ze_rs.at[k, c], nid)
+    def z_send(k, c, t):
+        b, s = (zs, zr) if k == 0 else (zs2, zr2)
+        return rc(b.at[t, :, cols(c)], s.at[z, :, cols(c)], z_ss.at[k, c, t], z_rs.at[k, c, z], {"row": t * 2 + x})
+
+    def z_recv(k, c, t):
+        b, s = (zs, zr) if k == 0 else (zs2, zr2)
+        return rc(b.at[t, :, cols(c)], s.at[t, :, cols(c)], z_ss.at[k, c, t], z_rs.at[k, c, t], {"row": t * 2 + x})
 
     def stage_a(k, c):
-        f, t = (pf, xr) if k == 0 else (pf2, xr2)
-        b, a = (zs, za) if k == 0 else (zs2, za2)
+        f, t, b = (pf, xr, zs) if k == 0 else (pf2, xr2, zs2)
         q = cols(c)
         x_copy(k, c).wait_recv()
-        sf[:, :, q] = f[:, x, :, q] + t[:, :, q].astype(F32)
-
-        @pl.when(is_end)
-        def _():
-            b[pl.ds(three, 3), :, q] = sf[pl.ds(three, 3), :, q].astype(BF)
-            in_copy(k, c).start()
-
-        @pl.when(is_mid)
-        def _():
-            in_copy(k, c).wait_recv()
-            m = pl.ds(far, 2)
-            b[m, :, q] = (sf[m, :, q] + a[m, :, q].astype(F32)).astype(BF)
-            mid_copy(k, c, far).start()
+        v = f[:, x, :, q] + t[:, :, q].astype(F32)
+        sf[:, :, q] = v
+        b[:, :, q] = v.astype(BF)
+        for o in others:
+            z_send(k, c, o).start()
 
     def stage_b(k, c, final):
-        b, a, m = (zs, za, zb) if k == 0 else (zs2, za2, zb2)
-        q = cols(c)
-
-        @pl.when(is_end)
-        def _():
-            out_copy(k, c).wait_recv()
-            final(c, sf[z, :, q] + a[z, :, q].astype(F32))
-
-        @pl.when(is_mid)
-        def _():
-            mid_copy(k, c, near).wait_recv()
-            b[end_b, :, q] = (sf[end_b, :, q] + m[end_b, :, q].astype(F32)).astype(BF)
-            out_copy(k, c).start()
-            final(c, sf[z, :, q] + a[z, :, q].astype(F32) + m[z, :, q].astype(F32))
+        s = zr if k == 0 else zr2
+        q = cols(c)
+        v = sf[z, :, q]
+        for o in others:
+            z_recv(k, c, o).wait_recv()
+            v = v + s[o, :, q].astype(F32)
+        final(c, v)
 
     def rs_drain(k):
         for c in range(NC):
             x_copy(k, c).wait_send()
-
-            @pl.when(is_end)
-            def _():
-                in_copy(k, c).wait_send()
-
-            @pl.when(is_mid)
-            def _():
-                mid_copy(k, c, far).wait_send()
-                out_copy(k, c).wait_send()
+            for o in others:
+                z_send(k, c, o).wait_send()
 
     for c in range(NC):
         q = cols(c)
@@ -205,13 +160,13 @@
 
     lax.fori_loop(0, nj, factors, 0)
 
-    def agz(c, t):
+    def agz_send(c, t):
+        b = dsf.at[r, :, cols(c)]
+        return rc(b, b, agz_ss.at[c, t], agz_rs.at[c, z], {"row": t * 2 + x})
+
+    def agz_recv(c, t):
         b = dsf.at[t * 2 + x, :, cols(c)]
-        return rc(b, b, agz_ss.at[c, t], agz_rs.at[c, t], nid)
-
-    def agm(c, t):
-        b = dsf.at[t * 2 + x, :, cols(c)]
-        return rc(b, b, agm_ss.at[c, t], agz_rs.at[c, t], mid)
+        return rc(b, b, agz_ss.at[c, t], agz_rs.at[c, t], {"row": t * 2 + x})
 
     def agx(c, t, src_x):
         b = dsf.at[t * 2 + src_x, :, cols(c)]
@@ -221,40 +176,22 @@
         q = cols(c)
         out_ref[:, q] = v.astype(BF)
         dsf[r, :, q] = (v - teacher_ref[:, q].astype(F32)).astype(BF)
-        agz(c, z).start()
-        pl.when(is_mid)(lambda: agm(c, z).start())
         agx(c, z, x).start()
+        for o in others:
+            agz_send(c, o).start()
 
     def stage_c(c):
-        @pl.when(is_end)
-        def _():
-            agz(c, nz).wait_recv()
-            agx(c, nz, x).start()
-            agz(c, far_m).wait_recv()
-            agx(c, far_m, x).start()
-            agz(c, far_e).wait_recv()
-            agx(c, far_e, x).start()
-
-        @pl.when(is_mid)
-        def _():
-            agz(c, nz).wait_recv()
-            agm(c, nz).start()
-            agx(c, nz, x).start()
-            agm(c, far_m).wait_recv()
-            agz(c, far_m).start()
-            agx(c, far_m, x).start()
-            agm(c, far_e).wait_recv()
-            agz(c, far_e).start()
-            agx(c, far_e, x).start()
-
-    for step in ORDER:
-        c = int(step[1])
-        if step[0] == "A":
-            stage_a(0, c)
-        elif step[0] == "B":
-            stage_b(0, c, student_final)
-        else:
-            stage_c(c)
+        for o in others:
+            agz_recv(c, o).wait_recv()
+            agx(c, o, x).start()
+
+    for i in range(NC + LAG_C):
+        if i < NC:
+            stage_a(0, i)
+        if 0 <= i - LAG_B < NC:
+            stage_b(0, i - LAG_B, student_final)
+        if 0 <= i - LAG_C < NC:
+            stage_c(i - LAG_C)
     for c in range(NC):
         for t in range(4):
             agx(c, t, 1 - x).wait_recv()
@@ -295,12 +232,11 @@
     def dtok_final(c, v):
         dtok_ref[:, cols(c)] = v.astype(BF)
 
-    for step in ORDER:
-        c = int(step[1])
-        if step[0] == "A":
-            stage_a(1, c)
-        elif step[0] == "B":
-            stage_b(1, c, dtok_final)
+    for i in range(NC + LAG_B):
+        if i < NC:
+            stage_a(1, i)
+        if i >= LAG_B:
+            stage_b(1, i - LAG_B, dtok_final)
 
     def drain(j, carry):
         gu_copy(j).wait_send()
@@ -311,16 +247,10 @@
     rs_drain(0)
     rs_drain(1)
     for c in range(NC):
-        agz(c, z).wait_send()
+        for o in others:
+            agz_send(c, o).wait_send()
         for t in range(4):
             agx(c, t, x).wait_send()
-
-        @pl.when(is_mid)
-        def _():
-            agm(c, z).wait_send()
-            agm(c, nz).wait_send()
-            agz(c, far_m).wait_send()
-            agz(c, far_e).wait_send()
 
     for i, (a, b) in enumerate(((hid, hid_h), (dsf, ds_h), (dg, dg_h), (du, du_h))):
         pltpu.make_async_copy(a, b, st.at[i]).wait()
@@ -333,7 +263,7 @@
     nj = ff // FCH
     V = pltpu.VMEM
     D = pltpu.SemaphoreType.DMA
-    rs_set = [V((4, rows, d), BF)] * 3
+    rs_set = [V((4, rows, d), BF)] * 2
     scratch = [
         V((m, d), BF), V((d, ff), BF), V((d, ff), BF), V((ff, d), BF),
         V((m, ff), F32), V((m, ff), F32),
@@ -345,8 +275,7 @@
         V((4, 2, rows, d), F32), V((4, 2, rows, d), BF), V((4, rows, d), BF), *rs_set,
         D, D((nj,)), D((nj,)), D((NC,)), D((4,)),
         D((nj,)), D((nj,)), D((nj,)), D((nj,)),
-        *([D((2, NC))] * 8),
-        *([D((NC, 4))] * 5),
+        *([D((2, NC))] * 2), *([D((2, NC, 4))] * 2), *([D((NC, 4))] * 4),
     ]
     hbm = pl.BlockSpec(memory_space=pl.ANY)
     vm = pl.BlockSpec(memory_space=pltpu.VMEM)
@@ -369,12 +298,46 @@
     )(tokens, teacher, gate_weight, up_weight, down_weight)
 
 
+def grads_kernel(tok, hid, ds, dg, du, gg, gu, gd):
+    t = tok[...]
+    gg[...] = tn(t, dg[...]).astype(BF)
+    gu[...] = tn(t, du[...]).astype(BF)
+    gd[...] = tn(hid[...], ds[...]).astype(BF)
+
+
+def weight_grads(tokens, hid, ds, dg, du):
+    m, d = tokens.shape
+    ff = hid.shape[1]
+    steps = 8
+    return pl.pallas_call(
+        grads_kernel,
+        grid=(steps,),
+        out_shape=(
+            jax.ShapeDtypeStruct((d, ff), BF), jax.ShapeDtypeStruct((d, ff), BF),
+            jax.ShapeDtypeStruct((ff, d), BF),
+        ),
+        in_specs=[
+            pl.BlockSpec((m, d // steps), lambda i: (0, i)),
+            pl.BlockSpec((m, ff // steps), lambda i: (0, i)),
+            pl.BlockSpec((m, d), lambda i: (0, 0)),
+            pl.BlockSpec((m, ff), lambda i: (0, 0)),
+            pl.BlockSpec((m, ff), lambda i: (0, 0)),
+        ],
+        out_specs=(
+            pl.BlockSpec((d // steps, ff), lambda i: (i, 0)),
+            pl.BlockSpec((d // steps, ff), lambda i: (i, 0)),
+            pl.BlockSpec((ff // steps, d), lambda i: (i, 0)),
+        ),
+        compiler_params=pltpu.CompilerParams(vmem_limit_bytes=60 * 1024 * 1024),
+        cost_estimate=pl.CostEstimate(flops=6 * m * d * ff, bytes_accessed=6 * d * ff, transcendentals=0),
+        name="weight_grads",
+    )(tokens, hid, ds, dg, du)
+
+
 def local_fused(tokens, teacher, gate_weight, up_weight, down_weight):
     out, dtok, hid, ds, dg, du = fused(tokens, teacher, gate_weight, up_weight, down_weight)
     ds = ds.reshape(tokens.shape)
-    grad_down = tn(hid, ds).astype(BF)
-    grad_gate = tn(tokens, dg).astype(BF)
-    grad_up = tn(tokens, du).astype(BF)
+    grad_gate, grad_up, grad_down = weight_grads(tokens, hid, ds, dg, du)
     return out, dtok, grad_gate, grad_up, grad_down
 
 

time: 154 us -> 91.5 us (0.59)
  local copies, waits for them, and re-layouts: 26 us -> 1.32 us
  Pallas kernels: 108 us -> 89.2 us
  matrix products: 18.6 us -> 0 us
    pallas_call x1, Pallas kernels: 108 us -> 77.1 us  [fused(): pl.pallas_call(kernel, out_shape=(jax.ShapeDtypeStruct((rows, d), BF), ja...]
    unnamed x16 -> x6, local copies, waits for them, and re-layouts: 26 us -> 1.32 us
    dot_general x3 -> x0, matrix products: 18.6 us -> none  [tn(): lax.dot_general(a, b, (((0,), (0,)), ((), ())), preferred_element_type=F32)]
    pallas_call x0 -> x1, Pallas kernels: none -> 12.2 us  [weight_grads(): pl.pallas_call(grads_kernel, grid=(steps,), out_shape=(jax.ShapeDtypeStru...]
where the time goes in v2:
time: 91.5 us; the launch traced here: 91.2 us
  Pallas kernels  89.2 us (97%)
  local copies, waits for them, and re-layouts  1.32 us (1%)
    pallas_call x1, Pallas kernels, fused(): pl.pallas_call(kernel, out_shape=(jax.ShapeDtypeStruct((rows, d), BF), ja...  77.1 us
    pallas_call x1, Pallas kernels, weight_grads(): pl.pallas_call(grads_kernel, grid=(steps,), out_shape=(jax.ShapeDtypeStru...  12.2 us

profile of v2, /device:TPU:0, one launch (start us, length us, event | category | flops | bytes accessed | tf_op | source)
XLA Modules:
  0.0 91.2 jit_solution(11882082281073954205)
XLA Ops:
  0.6 77.1 %chain.1 = (bf16[32,2048]{1,0:T(8,128)(2,1)}, bf16[32,2048]{1,0:T(8,128)(2,1)}, bf16[256,2048]{1,0:T(8,128)(2,1)}, bf16[8,32,2048]{2,1,0:T(8,128)(2,1)}, bf16[25...) custom-call(bf16[256,2048]{1,0:T(8,128)(2,1)} %tok.1, bf16[32,2048]{1,0:T(8,128)(2,1)} %teacher_ref.1, ...), custom_call_target="tpu_custom_call" | custom-call | flops 12884901888 | bytes 25165824 | tf_op jit(solution)/shard_map/chain/pallas_call | solution.py:283
  77.7 0.0 copy-start.1
  77.7 0.0 copy-start
  77.7 12.2 %weight_grads.1 = (bf16[2048,2048]{1,0:T(8,128)(2,1)}, bf16[2048,2048]{1,0:T(8,128)(2,1)}, bf16[2048,2048]{1,0:T(8,128)(2,1)}) custom-call(bf16[256,2048]{1,0:T(8,128)(2,1)} %tok.1, bf16[256,2048]{1,0:T(8,128)(2,1)} %get-tuple-element.16.hid, bf16[256,2048]{1,0:T(8,128)(2,1)} %bitcast.1, bf16[256,2048]{1,0:T(8,128)(2,1)} %get-tuple-element.18.dg, ...), custom_call_target="tpu_custom_call" | custom-call | flops 6442450944 | bytes 25165824 | tf_op jit(solution)/shard_map/weight_grads/pallas_call | solution.py:312
  89.9 0.0 copy-done.1
  89.9 0.7 copy.12
  90.6 0.0 copy-done
  90.6 0.7 copy.13
Async XLA Ops:
  77.7 12.2 %copy-start.1 = (bf16[32,2048]{1,0:T(8,128)(2,1)S(1)}, bf16[32,2048]{1,0:T(8,128)(2,1)}, u32[]{:S(2)}) copy-start(bf16[32,2048]{1,0:T(8,128)(2,1)} %get-tuple-element.28) | copy-start | bytes 393220
  77.7 12.8 %copy-start = (bf16[32,2048]{1,0:T(8,128)(2,1)S(1)}, bf16[32,2048]{1,0:T(8,128)(2,1)}, u32[]{:S(2)}) copy-start(bf16[32,2048]{1,0:T(8,128)(2,1)} %get-tuple-element.29) | copy-start | bytes 393220

commit v3 on v2

--- a/solution.py
+++ b/solution.py
@@ -8,7 +8,7 @@
 F32 = jnp.float32
 BF = jnp.bfloat16
 MESH = pl.DeviceIdType.MESH
-FCH = 512
+FCH = 1024
 NC = 4
 LAG_B = 1
 LAG_C = 2
@@ -308,7 +308,7 @@
 def weight_grads(tokens, hid, ds, dg, du):
     m, d = tokens.shape
     ff = hid.shape[1]
-    steps = 8
+    steps = 4
     return pl.pallas_call(
         grads_kernel,
         grid=(steps,),

time: 91.5 us -> 88.2 us (0.964)
  Pallas kernels: 89.2 us -> 85.6 us
    pallas_call x1, Pallas kernels: 77.1 us -> 74.3 us  [fused(): pl.pallas_call(kernel, out_shape=(jax.ShapeDtypeStruct((rows, d), BF), ja...]
    pallas_call x1, Pallas kernels: 12.2 us -> 11.2 us  [weight_grads(): pl.pallas_call(grads_kernel, grid=(steps,), out_shape=(jax.ShapeDtypeStru...]
where the time goes in v3:
time: 88.2 us; the launch traced here: 87.5 us
  Pallas kernels  85.6 us (97%)
  local copies, waits for them, and re-layouts  1.32 us (1%)
    pallas_call x1, Pallas kernels, fused(): pl.pallas_call(kernel, out_shape=(jax.ShapeDtypeStruct((rows, d), BF), ja...  74.3 us
    pallas_call x1, Pallas kernels, weight_grads(): pl.pallas_call(grads_kernel, grid=(steps,), out_shape=(jax.ShapeDtypeStru...  11.2 us

profile of v3, /device:TPU:0, one launch (start us, length us, event | category | flops | bytes accessed | tf_op | source)
XLA Modules:
  0.0 87.5 jit_solution(14188934157469071543)
XLA Ops:
  0.6 74.3 %chain.1 = (bf16[32,2048]{1,0:T(8,128)(2,1)}, bf16[32,2048]{1,0:T(8,128)(2,1)}, bf16[256,2048]{1,0:T(8,128)(2,1)}, bf16[8,32,2048]{2,1,0:T(8,128)(2,1)}, bf16[25...) custom-call(bf16[256,2048]{1,0:T(8,128)(2,1)} %tok.1, bf16[32,2048]{1,0:T(8,128)(2,1)} %teacher_ref.1, ...), custom_call_target="tpu_custom_call" | custom-call | flops 12884901888 | bytes 25165824 | tf_op jit(solution)/shard_map/chain/pallas_call | solution.py:283
  75.0 0.0 copy-start.1
  75.0 0.0 copy-start
  75.0 11.2 %weight_grads.1 = (bf16[2048,2048]{1,0:T(8,128)(2,1)}, bf16[2048,2048]{1,0:T(8,128)(2,1)}, bf16[2048,2048]{1,0:T(8,128)(2,1)}) custom-call(bf16[256,2048]{1,0:T(8,128)(2,1)} %tok.1, bf16[256,2048]{1,0:T(8,128)(2,1)} %get-tuple-element.16.hid, bf16[256,2048]{1,0:T(8,128)(2,1)} %bitcast.1, bf16[256,2048]{1,0:T(8,128)(2,1)} %get-tuple-element.18.dg, ...), custom_call_target="tpu_custom_call" | custom-call | flops 6442450944 | bytes 25165824 | tf_op jit(solution)/shard_map/weight_grads/pallas_call | solution.py:312
  86.2 0.0 copy-done.1
  86.2 0.7 copy.12
  86.9 0.0 copy-done
  86.9 0.7 copy.13
Async XLA Ops:
  75.0 11.3 %copy-start.1 = (bf16[32,2048]{1,0:T(8,128)(2,1)S(1)}, bf16[32,2048]{1,0:T(8,128)(2,1)}, u32[]{:S(2)}) copy-start(bf16[32,2048]{1,0:T(8,128)(2,1)} %get-tuple-element.28) | copy-start | bytes 393220
  75.0 11.9 %copy-start = (bf16[32,2048]{1,0:T(8,128)(2,1)S(1)}, bf16[32,2048]{1,0:T(8,128)(2,1)}, u32[]{:S(2)}) copy-start(bf16[32,2048]{1,0:T(8,128)(2,1)} %get-tuple-element.29) | copy-start | bytes 393220
